TPU v7x, 512 devices: a whole 4x8x8 slice. The times are simulated.
512 devices in a mesh: col: 8 (over y_lo, core), dev: 64 (over y_hi, z, x).
Axes of the slice: x: 4, y: 8 (y_hi: 2, y_lo: 4; y = y_hi * 4 + y_lo), z: 8, core: 2. Of those that a mesh axis runs over, the one named last changes fastest.
Arguments:
- factor_a: float32 [1536, 16, 512], P('dev'), may hold values from -1 to 1
- factor_b: float32 [1536, 64, 512], P('dev', 'col'), may hold values from -1 to 1
- factor_occ: float32 [1536, 16, 512], P('dev'), may hold values from -1 to 1
- singles_a: float32 [16, 16], replicated, may hold values from -1.5 to 1.5
- singles_b: float32 [16, 64], P(None, 'col'), may hold values from -1.5 to 1.5
- doubles: bfloat16 [512, 512, 256], P('col', 'dev'), may hold values from -0.023925781 to 0.023925781
- orbital_a: float32 [16], P('col'), may hold values from 0.2 to 3
- orbital_b: float32 [64], P('dev'), may hold values from 0.2 to 3
- orbital_occ: float32 [16], replicated, may hold values from -2 to -0.3
Outputs:
- update: float32 [16, 64, 256], P('col', 'dev')
All inputs are finite; a program needn't handle non-finite values.
Results may differ from a plain program's by a relative error of at most 0.0049.
Values may be sent and summed in bfloat16 or wider, within the bound.
A program may use at most 64 MiB of HBM per device.

v0:
```python
import jax
import jax.numpy as jnp
from jax import lax
from jax.sharding import PartitionSpec as P


def body(
    factor_a, factor_b, factor_occ, singles_a, singles_b, doubles, orbital_a, orbital_b, orbital_occ
):
    highest = lax.Precision.HIGHEST
    c_tile = doubles.shape[0]
    d_tile = doubles.shape[1]
    pair_count = doubles.shape[2]
    shard_rows = factor_a.shape[0]
    a_rows = factor_a.shape[1]
    d_groups = factor_b.shape[2] // d_tile
    col_index = lax.axis_index("col")
    occ_tile = lax.dynamic_slice_in_dim(factor_occ, col_index * c_tile, c_tile, 2)
    a_tile = lax.dynamic_slice_in_dim(factor_a, col_index * c_tile, c_tile, 2)
    dressed_a = (a_tile - jnp.einsum("ka,qkc->qac", singles_a, occ_tile, precision=highest)).astype(
        jnp.bfloat16
    )
    dressed_a = dressed_a.reshape(shard_rows, a_rows * c_tile)
    dressed_b = (
        factor_b - jnp.einsum("kb,qkd->qbd", singles_b, factor_occ, precision=highest)
    ).astype(jnp.bfloat16)
    rows_all = lax.all_gather(dressed_b, "col", axis=1, tiled=True)
    b_rows_all = rows_all.shape[1]
    grouped = rows_all.reshape(shard_rows, b_rows_all, d_groups, d_tile)
    grouped = jnp.transpose(grouped, (0, 2, 1, 3)).reshape(
        shard_rows, d_groups, b_rows_all * d_tile
    )
    moved = lax.all_to_all(grouped, "dev", split_axis=1, concat_axis=0, tiled=True)
    whole_b = moved.reshape(moved.shape[0], -1)
    b_rows_all = whole_b.shape[1] // d_tile
    contract_first = (((0,), (0,)), ((), ()))
    whole_a = lax.all_gather(dressed_a, "dev", axis=0, tiled=True)
    integral = lax.dot_general(whole_a, whole_b, contract_first, preferred_element_type=jnp.float32)
    integral = integral.astype(jnp.bfloat16).reshape(a_rows, c_tile, b_rows_all, d_tile)
    integral = jnp.transpose(integral, (0, 2, 1, 3)).reshape(a_rows * b_rows_all, c_tile * d_tile)
    partial_value = jnp.dot(
        integral, doubles.reshape(c_tile * d_tile, pair_count), preferred_element_type=jnp.float32
    )
    partial_value = partial_value.reshape(a_rows, b_rows_all, pair_count)
    reduced = lax.psum_scatter(partial_value, "dev", scatter_dimension=1, tiled=True)
    total = lax.psum_scatter(reduced, "col", scatter_dimension=0, tiled=True)
    pair_energy = (orbital_occ[:, None] + orbital_occ[None, :]).reshape(-1)
    denominator = orbital_a[:, None, None] + orbital_b[None, :, None] - pair_energy[None, None, :]
    return total / denominator


def solution(mesh):
    return jax.shard_map(
        body,
        mesh=mesh,
        in_specs=(
            P("dev", None, None),
            P("dev", "col", None),
            P("dev", None, None),
            P(),
            P(None, "col"),
            P("col", "dev", None),
            P("col"),
            P("dev"),
            P(),
        ),
        out_specs=P("col", "dev", None),
        check_vma=False,
    )
```

profile of v0, /device:TPU:1, one launch (start us, length us, event | category | flops | bytes accessed | tf_op | source)
XLA Modules:
  0.0 714.7 jit_solution(8249692002151963328)
XLA Ops:
  6.5 0.0 copy-start
  6.5 0.0 all-gather.5.cloned.1.call-start
  6.5 1.1 copy-done
  7.7 2.2 fusion.1
  9.9 0.0 all-gather.5.cloned.1.call-update
  9.9 0.0 all-gather.3.cloned.1.call-start
  10.0 1.4 fusion.3
  11.3 0.7 reshape.86
  12.1 0.0 all-gather.3.cloned.1.call-update
  12.1 0.0 reduce-scatter.2.cloned.1.call-start
  12.1 42.0 %all-gather.5.cloned.1.call-done = bf16[24,64,512]{2,1,0:T(8,128)(2,1)} async-done(((bf16[24,8,512]{2,1,0:T(8,128)(2,1)}), bf16[24,64,512]{2,1,0:T(8,128)(2,1)}) %all-gather.5.cloned.1.call-update) | async-done | bytes 1572880 | tf_op jit(solution)/shard_map/all_gather | solution.py:27
  54.2 4.1 copy.21
  58.3 5.4 copy.22
  63.7 3.9 copy.23
  67.6 53.7 %all_to_all.15 = bf16[24,64,512]{2,0,1:T(8,128)(2,1)} all-to-all(bf16[24,64,512]{2,0,1:T(8,128)(2,1)S(1)} %copy.23), channel_id=1, replica_groups=mesh['col'=8,'dev'=64] {'dev'}, dimensions={1} | all-to-all | bytes 3145728 | tf_op jit(solution)/shard_map/all_to_all | solution.py:33
  121.3 96.4 %all-gather.3.cloned.1.call-done = bf16[1536,1024]{1,0:T(8,128)(2,1)} async-done(((bf16[24,1024]{1,0:T(8,128)(2,1)}), bf16[1536,1024]{1,0:T(8,128)(2,1)}) %all-gather.3.cloned.1.call-update) | async-done | bytes 3145744 | tf_op jit(solution)/shard_map/all_gather | solution.py:37
  217.7 4.2 convolution_convert_fusion
  221.9 1.3 copy.24
  223.2 2.9 reshape.90
  226.2 0.0 copy-start.1
  226.2 6.6 copy.29
  232.7 0.0 copy-done.1
  232.7 0.0 copy-start.2
  232.7 0.0 copy-start.3
  232.7 6.8 convolution_bitcast_fusion
  239.6 0.0 reduce-scatter.2.cloned.1.call-update
  239.6 0.0 copy-done.2
  239.6 0.1 broadcast_add_fusion
  239.7 0.1 add.46
  240.4 1.3 dynamic-slice
  242.3 0.0 copy-done.3
  242.4 389.7 %reduce-scatter.2.cloned.1.call-done = f32[16,1,256]{2,0,1:T(8,128)} async-done(((f32[16,64,256]{2,0,1:T(8,128)}), f32[16,1,256]{2,0,1:T(8,128)}) %reduce-scatter.2.cloned.1.call-update) | async-done | bytes 16400 | tf_op jit(solution)/shard_map/reduce_scatter | solution.py:45
  632.1 0.7 copy.27
  632.8 74.7 %all-reduce = f32[16,1,256]{2,1,0:T(1,128)S(1)} all-reduce(f32[16,1,256]{2,1,0:T(1,128)S(1)} %copy.27), channel_id=3, replica_groups=mesh['col'=8,'dev'=64] {'col'}, use_global_device_ids=true, to_apply=%region_1.0.clone | all-reduce | flops 4096 | bytes 32768
  707.5 0.7 dynamic-slice_divide_fusion
  (1 shorter events, 0.0 us)
Async XLA Ops:
  6.5 1.1 copy-start
  6.5 47.6 %all-gather.5.cloned.1.call-start = ((), (), s32[]{:S(2)}) async-start(), calls=%async_computation.3 | async-start | bytes 1769472 | tf_op jit(solution)/shard_map/all_gather | solution.py:27
  9.9 207.8 %all-gather.3.cloned.1.call-start = ((), (), s32[]{:S(2)}) async-start(), calls=%async_computation.2 | async-start | bytes 3194880 | tf_op jit(solution)/shard_map/all_gather | solution.py:37
  12.1 620.0 %reduce-scatter.2.cloned.1.call-start = ((), (), s32[]{:S(2)}) async-start(), calls=%async_computation.4 | async-start | bytes 1064960 | tf_op jit(solution)/shard_map/reduce_scatter | solution.py:45
  226.2 6.6 copy-start.1
  232.7 6.8 copy-start.2
  232.7 9.6 %copy-start.3 = (f32[2]{0:T(128)S(1)}, f32[2]{0:T(128)}, u32[]{:S(2)}) copy-start(f32[2]{0:T(128)} %param.15) | copy-start | bytes 28
Sparse Core Ops, SparseCore 0:
  10.0 44.0 all-gather.4
  58.7 158.9 all-gather.2
  239.7 392.3 reduce-scatter.1
where the time goes:
time: 715 us
  waiting for transfers between devices  528 us (74%)
  blocking collectives  128 us (18%)
  local copies, waits for them, and re-layouts  28.2 us (4%)
  matrix products  14.5 us (2%)
  between operations  14.5 us (2%)
    reduce_scatter x1, waiting for transfers between devices, body(): lax.psum_scatter(partial_value, 'dev', scatter_dimension=1, tiled=True)  390 us
    all_gather x1, waiting for transfers between devices, body(): whole_a = lax.all_gather(dressed_a, 'dev', axis=0, tiled=True)  96.4 us
    unnamed x1, blocking collectives  74.7 us
    all_to_all x1, blocking collectives, body(): lax.all_to_all(grouped, 'dev', split_axis=1, concat_axis=0, tiled=True)  53.7 us
    all_gather x1, waiting for transfers between devices, body(): rows_all = lax.all_gather(dressed_b, 'col', axis=1, tiled=True)  42 us
  transfers between devices with their start and end apart: 3, of which 3 were waited for; matrix products, arithmetic and copies ran while one was open for 2% of the time, Pallas kernels for 0%

commit v1 on v0

--- a/solution.py
+++ b/solution.py
@@ -30,7 +30,9 @@
     grouped = jnp.transpose(grouped, (0, 2, 1, 3)).reshape(
         shard_rows, d_groups, b_rows_all * d_tile
     )
-    moved = lax.all_to_all(grouped, "dev", split_axis=1, concat_axis=0, tiled=True)
+    moved = jnp.concatenate(
+        lax.all_to_all(jnp.stack(jnp.split(grouped, lax.axis_size("dev"), 1), 0), "dev", 0, 0), 0
+    )
     whole_b = moved.reshape(moved.shape[0], -1)
     b_rows_all = whole_b.shape[1] // d_tile
     contract_first = (((0,), (0,)), ((), ()))

time: 715 us -> 809 us (1.13)
  local copies, waits for them, and re-layouts: 28.2 us -> 213 us
  waiting for transfers between devices: 528 us -> 430 us
    split x0 -> x4, local copies, waits for them, and re-layouts: none -> 189 us  [body(): jnp.split(grouped, lax.axis_size('dev'), 1)]
    all_gather x1, waiting for transfers between devices: 96.4 us -> 0.01 us  [body(): whole_a = lax.all_gather(dressed_a, 'dev', axis=0, tiled=True)]
  transfers between devices with their start and end apart: 3 -> 3, of which waited for: 3 -> 2; matrix products, arithmetic and copies ran while one was open for 2% -> 25% of each run, Pallas kernels for 0% -> 0%
where the time goes in v1:
time: 809 us; the launch traced here: 802 us
  waiting for transfers between devices  430 us (53%)
  local copies, waits for them, and re-layouts  213 us (26%)
  blocking collectives  129 us (16%)
  between operations  15.3 us (2%)
  matrix products  14.1 us (2%)
    reduce_scatter x1, waiting for transfers between devices, body(): lax.psum_scatter(partial_value, 'dev', scatter_dimension=1, tiled=True)  387 us
    split x4, local copies, waits for them, and re-layouts, body(): jnp.split(grouped, lax.axis_size('dev'), 1)  189 us
    unnamed x1, blocking collectives  75.2 us
    all_to_all x1, blocking collectives, body(): lax.all_to_all(jnp.stack(jnp.split(grouped, lax.axis_size('dev'), 1), 0),...  54 us
    all_gather x1, waiting for transfers between devices, body(): rows_all = lax.all_gather(dressed_b, 'col', axis=1, tiled=True)  42 us
  transfers between devices with their start and end apart: 3, of which 2 were waited for; matrix products, arithmetic and copies ran while one was open for 25% of the time, Pallas kernels for 0%

profile of v1, /device:TPU:1, one launch (start us, length us, event | category | flops | bytes accessed | tf_op | source)
XLA Modules:
  0.0 802.3 jit_solution(4617937562389698255)
XLA Ops:
  6.5 0.0 copy-start
  6.5 0.0 copy-start.2
  6.5 0.0 all-gather.5.cloned.1.call-start
  6.5 1.1 copy-done
  7.7 2.2 fusion.1
  9.9 0.0 all-gather.5.cloned.1.call-update
  9.9 0.0 all-gather.3.cloned.1.call-start
  10.0 0.0 copy-done.2
  10.0 1.3 fusion.3
  11.3 0.7 reshape.82
  12.1 0.0 all-gather.3.cloned.1.call-update
  12.1 0.0 reduce-scatter.2.cloned.1.call-start
  12.1 42.0 %all-gather.5.cloned.1.call-done = bf16[24,64,512]{2,1,0:T(8,128)(2,1)} async-done(((bf16[24,8,512]{2,1,0:T(8,128)(2,1)}), bf16[24,64,512]{2,1,0:T(8,128)(2,1)}) %all-gather.5.cloned.1.call-update) | async-done | bytes 1572880 | tf_op jit(solution)/shard_map/all_gather | solution.py:27
  54.2 4.1 copy.1658
  58.3 5.4 copy.1659
  63.7 21.9 %slice_reduce_fusion.57 = (bf16[24,512]{1,0:T(8,128)(2,1)S(1)}, bf16[24,512]{1,0:T(8,128)(2,1)S(1)}, bf16[24,512]{1,0:T(8,128)(2,1)S(1)}, bf16[24,512]{1,0:T(8,1...) fusion(bf16[24,64,512]{1,2,0:T(8,128)(2,1)} %bitcast.166), kind=kLoop, calls=%fused_computation.57 | loop fusion | bytes 344064 | tf_op jit(solution)/shard_map/split | solution.py:34
  85.6 55.8 %slice_reduce_fusion.38 = (bf16[24,512]{1,0:T(8,128)(2,1)S(1)}, bf16[24,512]{1,0:T(8,128)(2,1)S(1)}, bf16[24,512]{1,0:T(8,128)(2,1)S(1)}, bf16[24,512]{1,0:T(8,1...) fusion(bf16[24,64,512]{1,2,0:T(8,128)(2,1)} %bitcast.167), kind=kLoop, calls=%fused_computation.38 | loop fusion | bytes 933888 | tf_op jit(solution)/shard_map/split | solution.py:34
  141.5 55.5 %slice_reduce_fusion.19 = (bf16[24,512]{1,0:T(8,128)(2,1)S(1)}, bf16[24,512]{1,0:T(8,128)(2,1)S(1)}, bf16[24,512]{1,0:T(8,128)(2,1)S(1)}, bf16[24,512]{1,0:T(8,1...) fusion(bf16[24,64,512]{1,2,0:T(8,128)(2,1)} %bitcast.168), kind=kLoop, calls=%fused_computation.19 | loop fusion | bytes 933888 | tf_op jit(solution)/shard_map/split | solution.py:34
  197.0 55.5 %slice_reduce_fusion = (bf16[24,512]{1,0:T(8,128)(2,1)S(1)}, bf16[24,512]{1,0:T(8,128)(2,1)S(1)}, bf16[24,512]{1,0:T(8,128)(2,1)S(1)}, bf16[24,512]{1,0:T(8,128)...) fusion(bf16[24,64,512]{1,2,0:T(8,128)(2,1)} %bitcast.169), kind=kLoop, calls=%fused_computation | loop fusion | bytes 933888 | tf_op jit(solution)/shard_map/split | solution.py:34
  253.3 54.0 %all_to_all.5 = bf16[64,24,1,512]{3,1,2,0:T(8,128)(2,1)S(1)} all-to-all(bf16[64,24,1,512]{3,1,2,0:T(8,128)(2,1)S(1)} %constant_dynamic-update-slice_fusion), channel_id=1, replica_groups=mesh['col'=8,'dev'=64] {'dev'}, dimensions={0} | all-to-all | bytes 3145728 | tf_op jit(solution)/shard_map/all_to_all | solution.py:34
  307.2 0.0 all-gather.3.cloned.1.call-done
  307.2 3.7 convolution_convert_fusion
  310.9 1.3 copy.1660
  312.3 2.9 reshape.85
  315.2 0.0 copy-start.1
  315.2 6.5 copy.1665
  321.8 0.0 copy-done.1
  321.8 0.0 copy-start.3
  321.8 0.0 copy-start.4
  321.8 6.8 convolution_bitcast_fusion
  328.6 0.0 reduce-scatter.2.cloned.1.call-update
  328.6 0.0 copy-done.3
  328.7 0.1 broadcast_add_fusion
  328.7 0.1 add.46
  329.5 1.3 dynamic-slice
  331.4 0.0 copy-done.4
  331.4 387.4 %reduce-scatter.2.cloned.1.call-done = f32[16,1,256]{2,0,1:T(8,128)} async-done(((f32[16,64,256]{2,0,1:T(8,128)}), f32[16,1,256]{2,0,1:T(8,128)}) %reduce-scatter.2.cloned.1.call-update) | async-done | bytes 16400 | tf_op jit(solution)/shard_map/reduce_scatter | solution.py:47
  718.9 0.7 copy.1663
  719.6 75.2 %all-reduce = f32[16,1,256]{2,1,0:T(1,128)S(1)} all-reduce(f32[16,1,256]{2,1,0:T(1,128)S(1)} %copy.1663), channel_id=3, replica_groups=mesh['col'=8,'dev'=64] {'col'}, use_global_device_ids=true, to_apply=%region_1.0.clone | all-reduce | flops 4096 | bytes 32768
  794.8 0.7 dynamic-slice_divide_fusion
  (65 shorter events, 0.3 us)
Async XLA Ops:
  6.5 1.1 copy-start
  6.5 3.4 copy-start.2
  6.5 47.6 %all-gather.5.cloned.1.call-start = ((), (), s32[]{:S(2)}) async-start(), calls=%async_computation.3 | async-start | bytes 1769472 | tf_op jit(solution)/shard_map/all_gather | solution.py:27
  9.9 297.3 %all-gather.3.cloned.1.call-start = ((), (), s32[]{:S(2)}) async-start(), calls=%async_computation.2 | async-start | bytes 3194880 | tf_op jit(solution)/shard_map/all_gather | solution.py:39
  12.1 706.8 %reduce-scatter.2.cloned.1.call-start = ((), (), s32[]{:S(2)}) async-start(), calls=%async_computation.4 | async-start | bytes 1064960 | tf_op jit(solution)/shard_map/reduce_scatter | solution.py:47
  315.2 6.6 copy-start.1
  321.8 6.9 copy-start.3
  321.8 9.6 %copy-start.4 = (f32[2]{0:T(128)S(1)}, f32[2]{0:T(128)}, u32[]{:S(2)}) copy-start(f32[2]{0:T(128)} %param.15) | copy-start | bytes 28
Sparse Core Ops, SparseCore 0:
  10.0 44.0 all-gather.4
  58.7 140.5 all-gather.2
  328.8 390.0 reduce-scatter.1
